TPU v7x, 128 devices: a whole 4x4x4 slice. The times are simulated.
128 devices in a mesh: row: 16 (over z_hi, y, core), col: 8 (over z_lo, x).
Axes of the slice: x: 4, y: 4, z: 4 (z_hi: 2, z_lo: 2; z = z_hi * 2 + z_lo), core: 2. Of those that a mesh axis runs over, the one named last changes fastest.
Arguments:
- token_ids: int32 [16384], P(('row', 'col')), may hold values from 0 to 511
- embedding: bfloat16 [512, 8192], replicated, may hold values from -6 to 6
- norm_gain: bfloat16 [8192], replicated, may hold values from 0.099609375 to 1.8984375
- w_in: bfloat16 [8192, 12288], P(None, ('row', 'col')), may hold values from -0.0625 to 0.0625
- short_taps: float32 [7, 12288], replicated, may hold values from -2 to 2
- long_filter: float32 [16384, 4096], P(('row', 'col')), may hold values from -0.046875 to 0.046875
- skip_gain: float32 [4096], replicated, may hold values from -1 to 1
Outputs:
- mixed_out: bfloat16 [16384, 4096], P(('row', 'col'))
All inputs are finite; a program needn't handle non-finite values.
Results may differ from a plain program's by a relative error of at most 0.0095.
Values may be sent and summed in bfloat16 or wider, within the bound.
No kernel may reach another device: no remote copies, remote signals or barrier semaphores. Data moves between devices by JAX's collectives and lax.ppermute only.
A program may use at most 192 MiB of HBM per device.

v0:
```python
import math
import jax
import jax.numpy as jnp
from jax import lax
from jax.sharding import PartitionSpec as P

FFT_COLS = 128
EPSILON = 1e-05


def passed_along(x, axis, by):
    length = lax.axis_size(axis)
    pairs = [(i, i + by) for i in range(length) if 0 <= i + by < length]
    return lax.ppermute(x, axis, pairs)


def phase_table(first_index, second_index, period):
    turns = first_index * second_index % period
    return 2.0 * math.pi / period * turns.astype(jnp.float32)


def contract(form, table_part, data_part):
    return jnp.einsum(form, table_part, data_part, precision=lax.Precision.HIGHEST)


def project_table(embedding, norm_gain, w_in):
    rows_f32 = embedding.astype(jnp.float32)
    inverse_rms = lax.rsqrt(jnp.mean(rows_f32 * rows_f32, axis=1, keepdims=True) + EPSILON)
    normed = (rows_f32 * inverse_rms * norm_gain.astype(jnp.float32)).astype(jnp.bfloat16)
    own_columns = jnp.dot(normed, w_in, preferred_element_type=jnp.float32).astype(jnp.bfloat16)
    return lax.all_gather(own_columns, ("row", "col"), axis=1, tiled=True)


def short_filter(mixed_rows, short_taps):
    tap_count = short_taps.shape[0]
    row_count = mixed_rows.shape[0]
    earlier = passed_along(mixed_rows[row_count - (tap_count - 1) :], ("row", "col"), 1)
    extended = jnp.concatenate([earlier, mixed_rows], axis=0).astype(jnp.float32)
    result = short_taps[0] * extended[tap_count - 1 :]
    for offset in range(1, tap_count):
        begin_at = tap_count - 1 - offset
        result = result + short_taps[offset] * extended[begin_at : begin_at + row_count]
    return result


def local_causal(signal_all, filter_all):
    seq_len = signal_all.shape[0]
    width = signal_all.shape[1]
    short_len = seq_len // FFT_COLS
    first_len = 2 * short_len
    total_len = first_len * FFT_COLS
    angle_one = phase_table(
        lax.iota(jnp.int32, short_len)[:, None], lax.iota(jnp.int32, first_len)[None, :], first_len
    )
    cos_one = jnp.cos(angle_one)
    sin_one = jnp.sin(angle_one)
    angle_twist = phase_table(
        lax.iota(jnp.int32, first_len)[:, None], lax.iota(jnp.int32, FFT_COLS)[None, :], total_len
    )
    cos_twist = jnp.cos(angle_twist)
    sin_twist = jnp.sin(angle_twist)
    angle_two = phase_table(
        lax.iota(jnp.int32, FFT_COLS)[:, None], lax.iota(jnp.int32, FFT_COLS)[None, :], FFT_COLS
    )
    cos_two = jnp.cos(angle_two)
    sin_two = jnp.sin(angle_two)

    def forward(series):
        blocked = series.reshape(short_len, FFT_COLS, width)
        real_part = contract("sk,sjc->ckj", cos_one, blocked)
        imag_part = -contract("sk,sjc->ckj", sin_one, blocked)
        turned_re = real_part * cos_twist + imag_part * sin_twist
        turned_im = imag_part * cos_twist - real_part * sin_twist
        out_re = contract("jm,ckj->ckm", cos_two, turned_re) + contract(
            "jm,ckj->ckm", sin_two, turned_im
        )
        out_im = contract("jm,ckj->ckm", cos_two, turned_im) - contract(
            "jm,ckj->ckm", sin_two, turned_re
        )
        return (out_re, out_im)

    signal_re, signal_im = forward(signal_all)
    filter_re, filter_im = forward(filter_all)
    product_re = signal_re * filter_re - signal_im * filter_im
    product_im = signal_re * filter_im + signal_im * filter_re
    back_re = contract("jm,ckm->ckj", cos_two, product_re) - contract(
        "jm,ckm->ckj", sin_two, product_im
    )
    back_im = contract("jm,ckm->ckj", cos_two, product_im) + contract(
        "jm,ckm->ckj", sin_two, product_re
    )
    turned_re = back_re * cos_twist - back_im * sin_twist
    turned_im = back_im * cos_twist + back_re * sin_twist
    summed = contract("sk,ckj->sjc", cos_one, turned_re) - contract(
        "sk,ckj->sjc", sin_one, turned_im
    )
    return (summed * (1.0 / total_len)).reshape(seq_len, width)


def local(token_ids, embedding, norm_gain, w_in, short_taps, long_filter, skip_gain):
    lookup_table = project_table(embedding, norm_gain, w_in)
    vocab_size = lookup_table.shape[0]
    one_hot = (token_ids[:, None] == lax.iota(jnp.int32, vocab_size)[None, :]).astype(jnp.bfloat16)
    mixed_rows = jnp.dot(one_hot, lookup_table, preferred_element_type=jnp.float32).astype(
        jnp.bfloat16
    )
    filtered = short_filter(mixed_rows, short_taps)
    channels = filtered.shape[1] // 3
    gate_out = filtered[:, :channels]
    signal = filtered[:, channels : 2 * channels] * filtered[:, 2 * channels :]
    signal_all, filter_all = (
        lax.all_to_all(signal, ("row", "col"), split_axis=1, concat_axis=0, tiled=True),
        lax.all_to_all(long_filter, ("row", "col"), split_axis=1, concat_axis=0, tiled=True),
    )
    causal_all = local_causal(signal_all, filter_all)
    long_part = lax.all_to_all(causal_all, ("row", "col"), split_axis=0, concat_axis=1, tiled=True)
    mixed_out = gate_out * (long_part + skip_gain * signal)
    return mixed_out.astype(jnp.bfloat16)


def solution(mesh):
    in_specs = (
        P(("row", "col")),
        P(),
        P(),
        P(None, ("row", "col")),
        P(),
        P(("row", "col"), None),
        P(),
    )
    out_specs = P(("row", "col"), None)
    return jax.shard_map(local, mesh=mesh, in_specs=in_specs, out_specs=out_specs, check_vma=False)
```

profile of v0, /device:TPU:0, one launch (start us, length us, event | category | flops | bytes accessed | tf_op | source)
XLA Modules:
  0.0 561.6 jit_solution(3965734877258306150)
XLA Ops:
  6.5 5.3 fusion
  19.5 11.7 %all-to-all-start.1 = ((f32[128,128,32]{0,2,1:T(8,128)}), f32[128,128,32]{0,2,1:T(8,128)}, u32[]{:S(2)}, u32[]{:S(2)}) async-start(f32[128,128,32]{0,2,1:T(8,128)} %bitcast.114), calls=%async_computation.1 | async-start | bytes 4194304 | tf_op jit(solution)/shard_map/all_to_all | solution.py:113
  32.2 30.5 %all-to-all-done.1 = f32[128,128,32]{0,2,1:T(8,128)} async-done(((f32[128,128,32]{0,2,1:T(8,128)}), f32[128,128,32]{0,2,1:T(8,128)}, u32[]{:S(2)}, u32[]{:S(2)}) %all-to-all-start.1) | async-done | bytes 2097184 | tf_op jit(solution)/shard_map/all_to_all | solution.py:113
  62.7 9.3 %fusion.38 = f32[256,128,32]{1,0,2:T(8,128)} fusion(f32[128,128,32]{0,2,1:T(8,128)} %all-to-all-done.1), kind=kOutput, calls=%fused_computation.58 | convolution fusion | flops 1611071488 | bytes 6291456 | tf_op jit(solution)/shard_map/sk,sjc->ckj/dot_general | solution.py:23
  71.9 281.6 %all-gather.2.cloned.1.call-done = bf16[512,12288]{0,1:T(8,128)(2,1)} async-done(((bf16[512,96]{0,1:T(8,128)(2,1)}), bf16[512,12288]{0,1:T(8,128)(2,1)}) %all-gather.2.cloned.1.call-update) | async-done | bytes 12582928 | tf_op jit(solution)/shard_map/all_gather | solution.py:31
  353.6 8.8 %convolution_convert_fusion = bf16[128,12288]{1,0:T(8,128)(2,1)S(1)} fusion(bf16[512,12288]{0,1:T(8,128)(2,1)} %all-gather.2.cloned.1.call-done, s32[128]{0:T(128)S(1)} %copy-done.10), kind=kOutput, calls=%fused_computation.5 | convolution fusion | flops 1612251136 | bytes 15729152 | tf_op jit(solution)/shard_map/dot_general | solution.py:104
  366.3 9.3 %fusion.40 = f32[256,128,32]{1,0,2:T(8,128)} fusion(f32[128,128,32]{0,2,1:T(8,128)} %all-to-all-done.1), kind=kOutput, calls=%fused_computation.60 | convolution fusion | flops 1611071488 | bytes 6291456 | tf_op jit(solution)/shard_map/sk,sjc->ckj/dot_general | solution.py:23
  376.5 5.2 fusion.7
  388.8 11.1 %all-to-all-start = ((f32[128,128,32]{0,2,1:T(8,128)}), f32[128,128,32]{0,2,1:T(8,128)}, u32[]{:S(2)}, u32[]{:S(2)}) async-start(f32[128,128,32]{0,2,1:T(8,128)} %bitcast.115), calls=%async_computation | async-start | bytes 4194304 | tf_op jit(solution)/shard_map/all_to_all | solution.py:112
  399.9 6.8 %fusion.13 = f32[32,256,128]{2,1,0:T(8,128)S(1)} fusion(f32[256,128,32]{1,0,2:T(8,128)} %fusion.40, f32[256,128,32]{1,0,2:T(8,128)} %fusion.38, f32[256,128]{1,0:T(8,128)S(1)} %copy.49, f32[256,128]{1,0:T(8,128)S(1)} %copy.47), kind=kOutput, calls=%fused_computation.22 | convolution fusion | flops 1615036416 | bytes 12845056 | tf_op jit(solution)/shard_map/jm,ckj->ckm/dot_general | solution.py:23
  406.7 4.2 fusion.15
  410.9 5.8 %fusion.34 = f32[32,256,128]{2,1,0:T(8,128)} fusion(f32[32,256,128]{2,1,0:T(8,128)S(1)} %fusion.13, f32[256,128,32]{1,0,2:T(8,128)S(1)} %copy-done.3, f32[256,128,32]{1,0,2:T(8,128)S(1)} %copy-done.2, f32[256,128]{1,0:T(8,128)S(1)} %copy.49, f32[256,128]{1,0:T(8,128)S(1)} %copy.47), kind=kOutput, calls=%fused_computation.50 | convolution fusion | flops 1616084992 | bytes 17039360 | tf_op jit(solution)/shard_map/jm,ckj->ckm/dot_general | solution.py:23
  416.7 5.8 %fusion.31 = f32[32,256,128]{2,1,0:T(8,128)} fusion(f32[32,256,128]{2,1,0:T(8,128)S(1)} %fusion.15, f32[256,128,32]{1,0,2:T(8,128)S(1)} %copy-done.3, f32[256,128,32]{1,0,2:T(8,128)S(1)} %copy-done.2, f32[256,128]{1,0:T(8,128)S(1)} %copy.49, f32[256,128]{1,0:T(8,128)S(1)} %copy.47), kind=kOutput, calls=%fused_computation.49 | convolution fusion | flops 1616084992 | bytes 17039360 | tf_op jit(solution)/shard_map/jm,ckj->ckm/dot_general | solution.py:23
  422.5 6.8 %all-to-all-done = f32[128,128,32]{0,2,1:T(8,128)} async-done(((f32[128,128,32]{0,2,1:T(8,128)}), f32[128,128,32]{0,2,1:T(8,128)}, u32[]{:S(2)}, u32[]{:S(2)}) %all-to-all-start) | async-done | bytes 2097184 | tf_op jit(solution)/shard_map/all_to_all | solution.py:112
  432.5 5.7 %fusion.42 = f32[128,32,256]{2,0,1:T(8,128)S(1)} fusion(f32[128,128,32]{1,0,2:T(8,128)} %copy.41), kind=kOutput, calls=%fused_computation.62 | convolution fusion | flops 1611071488 | bytes 6291456 | tf_op jit(solution)/shard_map/sk,sjc->ckj/dot_general | solution.py:23
  442.2 9.4 %fusion.57 = f32[32,256,128]{2,1,0:T(8,128)} fusion(f32[128,32,256]{2,0,1:T(8,128)S(1)} %fusion.44, f32[128,32,256]{2,0,1:T(8,128)S(1)} %fusion.42, f32[256,128]{0,1:T(8,128)S(1)} %get-tuple-element.14, f32[256,128]{0,1:T(8,128)S(1)} %get-tuple-element.15), kind=kOutput, calls=%fused_computation.74 | convolution fusion | flops 1615036416 | bytes 12845056 | tf_op jit(solution)/shard_map/jm,ckj->ckm/dot_general | solution.py:23
  451.6 7.4 %fusion.61 = f32[32,256,128]{2,1,0:T(8,128)S(1)} fusion(f32[128,32,256]{2,0,1:T(8,128)S(1)} %fusion.44, f32[128,32,256]{2,0,1:T(8,128)S(1)} %fusion.42, f32[256,128]{0,1:T(8,128)S(1)} %get-tuple-element.14, f32[256,128]{0,1:T(8,128)S(1)} %get-tuple-element.15), kind=kOutput, calls=%fused_computation.75 | convolution fusion | flops 1615036416 | bytes 12845056 | tf_op jit(solution)/shard_map/jm,ckj->ckm/dot_general | solution.py:23
  459.0 9.1 %convolution_add_fusion.1 = f32[32,256,128]{2,1,0:T(8,128)} fusion(f32[32,256,128]{2,1,0:T(8,128)S(1)} %fusion.61, f32[128,32,256]{2,0,1:T(8,128)S(1)} %fusion.44, f32[128,32,256]{2,0,1:T(8,128)S(1)} %fusion.42, f32[256,128]{0,1:T(8,128)S(1)} %get-tuple-element.14, f32[256,128]{0,1:T(8,128)S(1)} %get-tuple-element.15), kind=kOutput, calls=%fused_computation.54 | convolution fusion | flops 1616084992 | bytes 17039360 | tf_op jit(solution)/shard_map/jm,ckj->ckm/dot_general | solution.py:23
  468.1 11.9 %multiply_add_fusion = (f32[32,256,128]{2,1,0:T(8,128)S(1)}, f32[32,256,128]{2,1,0:T(8,128)S(1)}) fusion(f32[32,256,128]{2,1,0:T(8,128)} %fusion.31, f32[32,256,128]{2,1,0:T(8,128)} %convolution_add_fusion.1, f32[32,256,128]{2,1,0:T(8,128)} %fusion.34, f32[32,256,128]{2,1,0:T(8,128)} %fusion.57, f32[128,32,256]{2,0,1:T(8,128)S(1)} %fusion.44, ...), kind=kOutput, calls=%fused_computation.44 | convolution fusion | flops 1622376448 | bytes 33816576 | tf_op jit(solution)/shard_map/jm,ckj->ckm/dot_general | solution.py:23
  488.4 4.9 convolution_add_fusion
  493.3 4.2 convolution_subtract_fusion
  501.7 5.8 %multiply_bitcast_fusion = f32[128,128,32]{0,1,2:T(8,128)} fusion(f32[32,128,128]{2,1,0:T(8,128)S(1)} %fusion.23, f32[32,256,128]{1,2,0:T(8,128)S(1)} %convolution_add_fusion, f32[32,256,128]{1,2,0:T(8,128)S(1)} %convolution_subtract_fusion, f32[256,128]{0,1:T(8,128)S(1)} %get-tuple-element.14, f32[256,128]{0,1:T(8,128)S(1)} %get-tuple-element.15), kind=kOutput, calls=%fused_computation.66 | convolution fusion | flops 1615265792 | bytes 12845056 | tf_op jit(solution)/shard_map/sk,ckj->sjc/dot_general | solution.py:23
  510.7 35.6 %all_to_all.48 = f32[128,128,32]{1,2,0:T(8,128)} all-to-all(f32[128,128,32]{1,2,0:T(8,128)} %copy.56), channel_id=1, replica_groups=mesh['row'=16,'col'=8] {'row','col'}, dimensions={0} | all-to-all | bytes 4194304 | tf_op jit(solution)/shard_map/all_to_all | solution.py:116
  549.2 5.0 fusion.37
  (45 shorter events, 46.4 us)
Async XLA Ops:
  6.5 5.3 copy-start
  6.5 5.3 copy-start.9
  6.5 347.0 %all-gather.2.cloned.1.call-start = ((), (), s32[]{:S(2)}) async-start(), calls=%async_computation.3 | async-start | bytes 12681216 | tf_op jit(solution)/shard_map/all_gather | solution.py:31
  6.5 6.3 %copy-start.6 = (bf16[512,8192]{1,0:T(8,128)(2,1)S(1)}, bf16[512,8192]{1,0:T(8,128)(2,1)}, u32[]{:S(2)}) copy-start(bf16[512,8192]{1,0:T(8,128)(2,1)} %param.8) | copy-start | bytes 25165828
  16.5 15.4 %copy-start.7 = (f32[7,12288]{1,0:T(8,128)S(1)}, f32[7,12288]{1,0:T(8,128)}, u32[]{:S(2)}) copy-start(f32[7,12288]{1,0:T(8,128)} %param.11) | copy-start | bytes 1032196
  19.5 43.2 %all-to-all-start.1 = ((f32[128,128,32]{0,2,1:T(8,128)}), f32[128,128,32]{0,2,1:T(8,128)}, u32[]{:S(2)}, u32[]{:S(2)}) async-start(f32[128,128,32]{0,2,1:T(8,128)} %bitcast.114), calls=%async_computation.1 | async-start | bytes 4194304 | tf_op jit(solution)/shard_map/all_to_all | solution.py:113
  31.2 322.4 %copy-start.10 = (s32[128]{0:T(128)S(1)}, s32[128]{0:T(128)}, u32[]{:S(2)}) copy-start(s32[128]{0:T(128)} %param.7) | copy-start | bytes 1540
  362.4 13.2 %collective-permute-start = (bf16[6,12288]{1,0:T(8,128)(2,1)S(1)}, bf16[6,12288]{1,0:T(8,128)(2,1)S(1)}, u32[]{:S(2)}, u32[]{:S(2)}) collective-permute-start(bf16[6,12288]{1,0:T(8,128)(2,1)S(1)} %slice.72), channel_id=1, source_target_pairs={{0,1},{1,2},{2,3},{3,4},{4,5},{5,6},{6,7},{7,8},{8,9},{9,10},{10,1... | collective-permute-start | bytes 442376 | tf_op jit(solution)/shard_map/ppermute | solution.py:14
  381.7 2.7 copy-start.4
  388.8 40.5 %all-to-all-start = ((f32[128,128,32]{0,2,1:T(8,128)}), f32[128,128,32]{0,2,1:T(8,128)}, u32[]{:S(2)}, u32[]{:S(2)}) async-start(f32[128,128,32]{0,2,1:T(8,128)} %bitcast.115), calls=%async_computation | async-start | bytes 4194304 | tf_op jit(solution)/shard_map/all_to_all | solution.py:112
  399.9 6.8 %copy-start.2 = (f32[256,128,32]{1,0,2:T(8,128)S(1)}, f32[256,128,32]{1,0,2:T(8,128)}, u32[]{:S(2)}) copy-start(f32[256,128,32]{1,0,2:T(8,128)} %fusion.38) | copy-start | bytes 12582916
  399.9 6.8 %copy-start.3 = (f32[256,128,32]{1,0,2:T(8,128)S(1)}, f32[256,128,32]{1,0,2:T(8,128)}, u32[]{:S(2)}) copy-start(f32[256,128,32]{1,0,2:T(8,128)} %fusion.40) | copy-start | bytes 12582916
  432.4 5.7 %copy-start.5 = (f32[128,128,32]{1,0,2:T(8,128)S(1)}, f32[128,128,32]{1,0,2:T(8,128)}, u32[]{:S(2)}) copy-start(f32[128,128,32]{1,0,2:T(8,128)} %copy.41) | copy-start | bytes 6291460
  510.7 38.6 %copy-start.8 = (f32[4096]{0:T(1024)S(1)}, f32[4096]{0:T(1024)}, u32[]{:S(2)}) copy-start(f32[4096]{0:T(1024)} %param.13) | copy-start | bytes 49156
  546.2 8.1 %copy-start.1 = (bf16[8192,96]{0,1:T(8,128)(2,1)S(1)}, bf16[8192,96]{0,1:T(8,128)(2,1)}, u32[]{:S(2)}) copy-start(bf16[8192,96]{0,1:T(8,128)(2,1)} %param.10) | copy-start | bytes 4718596
Sparse Core Ops, SparseCore 0:
  16.6 336.8 all-gather.1
where the time goes:
time: 571 us; the launch traced here: 562 us
  waiting for transfers between devices  319 us (56%)
  matrix products  129 us (23%)
  blocking collectives  35.6 us (6%)
  starting transfers between devices  26.6 us (5%)
  local copies, waits for them, and re-layouts  19.3 us (3%)
  other arithmetic  18.4 us (3%)
  between operations  14.1 us (2%)
    all_gather x1, waiting for transfers between devices, project_table(): return lax.all_gather(own_columns, ('row', 'col'), axis=1, tiled=True)  282 us
    dot_general x18, matrix products, contract(): jnp.einsum(form, table_part, data_part, precision=lax.Precision.HIGHEST)  116 us
    all_to_all x1, blocking collectives, local(): lax.all_to_all(causal_all, ('row', 'col'), split_axis=0, concat_axis=1, t...  35.6 us
    all_to_all x1, waiting for transfers between devices, local(): lax.all_to_all(long_filter, ('row', 'col'), split_axis=1, concat_axis=0,...  30.5 us
    all_to_all x1, starting transfers between devices, local(): lax.all_to_all(long_filter, ('row', 'col'), split_axis=1, concat_axis=0,...  11.7 us
  transfers between devices with their start and end apart: 4, of which 3 were waited for; matrix products, arithmetic and copies ran while one was open for 8% of the time, Pallas kernels for 0%

commit v1 on v0

--- a/solution.py
+++ b/solution.py
@@ -109,7 +109,15 @@
     gate_out = filtered[:, :channels]
     signal = filtered[:, channels : 2 * channels] * filtered[:, 2 * channels :]
     signal_all, filter_all = (
-        lax.all_to_all(signal, ("row", "col"), split_axis=1, concat_axis=0, tiled=True),
+        jnp.concatenate(
+            lax.all_to_all(
+                jnp.stack(jnp.split(signal, lax.axis_size(("row", "col")), axis=1)),
+                ("row", "col"),
+                0,
+                0,
+            ),
+            axis=0,
+        ),
         lax.all_to_all(long_filter, ("row", "col"), split_axis=1, concat_axis=0, tiled=True),
     )
     causal_all = local_causal(signal_all, filter_all)

time: 571 us -> 815 us (1.43)
  local copies, waits for them, and re-layouts: 19.3 us -> 259 us
    another operation x0 -> x136, local copies, waits for them, and re-layouts: none -> 136 us  [local(): jnp.stack(jnp.split(signal, lax.axis_size(('row', 'col')), axis=1))]
    unnamed x23 -> x230, local copies, waits for them, and re-layouts: 6.64 us -> 114 us
  transfers between devices with their start and end apart: 4 -> 4, of which waited for: 3 -> 3; matrix products, arithmetic and copies ran while one was open for 8% -> 6% of each run, Pallas kernels for 0% -> 0%
where the time goes in v1:
time: 815 us; the launch traced here: 800 us
  waiting for transfers between devices  318 us (39%)
  local copies, waits for them, and re-layouts  259 us (32%)
  matrix products  129 us (16%)
  blocking collectives  35.4 us (4%)
  starting transfers between devices  27.1 us (3%)
  other arithmetic  17.2 us (2%)
  between operations  14.4 us (2%)
    all_gather x1, waiting for transfers between devices, project_table(): return lax.all_gather(own_columns, ('row', 'col'), axis=1, tiled=True)  281 us
    another operation x136, local copies, waits for them, and re-layouts, local(): jnp.stack(jnp.split(signal, lax.axis_size(('row', 'col')), axis=1))  136 us
    dot_general x18, matrix products, contract(): jnp.einsum(form, table_part, data_part, precision=lax.Precision.HIGHEST)  116 us
    unnamed x230, local copies, waits for them, and re-layouts  114 us
    all_to_all x1, blocking collectives, local(): lax.all_to_all(causal_all, ('row', 'col'), split_axis=0, concat_axis=1, t...  35.4 us
    all_to_all x1, waiting for transfers between devices, local(): lax.all_to_all(long_filter, ('row', 'col'), split_axis=1, concat_axis=0,...  30.5 us
  transfers between devices with their start and end apart: 4, of which 3 were waited for; matrix products, arithmetic and copies ran while one was open for 6% of the time, Pallas kernels for 0%

profile of v1, /device:TPU:0, one launch (start us, length us, event | category | flops | bytes accessed | tf_op | source)
XLA Modules:
  0.0 800.4 jit_solution(3122146740892923633)
XLA Ops:
  6.5 5.3 fusion
  19.4 11.7 %all-to-all-start.1 = ((f32[128,128,32]{0,2,1:T(8,128)}), f32[128,128,32]{0,2,1:T(8,128)}, u32[]{:S(2)}, u32[]{:S(2)}) async-start(f32[128,128,32]{0,2,1:T(8,128)} %bitcast.366), calls=%async_computation.1 | async-start | bytes 4194304 | tf_op jit(solution)/shard_map/all_to_all | solution.py:121
  32.1 30.5 %all-to-all-done.1 = f32[128,128,32]{0,2,1:T(8,128)} async-done(((f32[128,128,32]{0,2,1:T(8,128)}), f32[128,128,32]{0,2,1:T(8,128)}, u32[]{:S(2)}, u32[]{:S(2)}) %all-to-all-start.1) | async-done | bytes 2097184 | tf_op jit(solution)/shard_map/all_to_all | solution.py:121
  62.6 9.3 %fusion.38 = f32[256,128,32]{1,0,2:T(8,128)} fusion(f32[128,128,32]{0,2,1:T(8,128)} %all-to-all-done.1), kind=kOutput, calls=%fused_computation.58 | convolution fusion | flops 1611071488 | bytes 6291456 | tf_op jit(solution)/shard_map/sk,sjc->ckj/dot_general | solution.py:23
  71.9 281.2 %all-gather.2.cloned.1.call-done = bf16[512,12288]{0,1:T(8,128)(2,1)} async-done(((bf16[512,96]{0,1:T(8,128)(2,1)}), bf16[512,12288]{0,1:T(8,128)(2,1)}) %all-gather.2.cloned.1.call-update) | async-done | bytes 12582928 | tf_op jit(solution)/shard_map/all_gather | solution.py:31
  353.1 8.8 %convolution_convert_fusion = bf16[128,12288]{1,0:T(8,128)(2,1)S(1)} fusion(bf16[512,12288]{0,1:T(8,128)(2,1)} %all-gather.2.cloned.1.call-done, s32[128]{0:T(128)S(1)} %copy-done.50), kind=kOutput, calls=%fused_computation.5 | convolution fusion | flops 1612251136 | bytes 15729152 | tf_op jit(solution)/shard_map/dot_general | solution.py:104
  365.9 9.4 %fusion.40 = f32[256,128,32]{1,0,2:T(8,128)} fusion(f32[128,128,32]{0,2,1:T(8,128)} %all-to-all-done.1), kind=kOutput, calls=%fused_computation.60 | convolution fusion | flops 1611071488 | bytes 6291456 | tf_op jit(solution)/shard_map/sk,sjc->ckj/dot_general | solution.py:23
  376.2 5.2 fusion.7
  627.3 11.5 %all-to-all-start = ((f32[128,128,32]{1,2,0:T(8,128)}), f32[128,128,32]{1,2,0:T(8,128)}, u32[]{:S(2)}, u32[]{:S(2)}) async-start(f32[128,128,32]{1,2,0:T(8,128)} %constant_dynamic-update-slice_fusion), calls=%async_computation | async-start | bytes 4194304 | tf_op jit(solution)/shard_map/all_to_all | solution.py:113
  638.7 6.8 fusion.13
  645.5 4.2 fusion.15
  649.8 5.8 fusion.34
  655.6 5.8 fusion.31
  661.4 6.7 all-to-all-done
  671.3 5.7 fusion.67
  681.0 9.4 %fusion.53 = f32[32,256,128]{2,1,0:T(8,128)} fusion(f32[128,32,256]{2,0,1:T(8,128)S(1)} %fusion.71, f32[128,32,256]{2,0,1:T(8,128)S(1)} %fusion.67, f32[256,128]{0,1:T(8,128)S(1)} %get-tuple-element.142, f32[256,128]{0,1:T(8,128)S(1)} %get-tuple-element.143), kind=kOutput, calls=%fused_computation.70 | convolution fusion | flops 1615036416 | bytes 12845056 | tf_op jit(solution)/shard_map/jm,ckj->ckm/dot_general | solution.py:23
  690.4 7.4 fusion.57
  697.8 9.2 %convolution_add_fusion.1 = f32[32,256,128]{2,1,0:T(8,128)} fusion(f32[32,256,128]{2,1,0:T(8,128)S(1)} %fusion.57, f32[128,32,256]{2,0,1:T(8,128)S(1)} %fusion.71, f32[128,32,256]{2,0,1:T(8,128)S(1)} %fusion.67, f32[256,128]{0,1:T(8,128)S(1)} %get-tuple-element.142, f32[256,128]{0,1:T(8,128)S(1)} %get-tuple-element.143), kind=kOutput, calls=%fused_computation.54 | convolution fusion | flops 1616084992 | bytes 17039360 | tf_op jit(solution)/shard_map/jm,ckj->ckm/dot_general | solution.py:23
  707.0 11.9 %multiply_add_fusion = (f32[32,256,128]{2,1,0:T(8,128)S(1)}, f32[32,256,128]{2,1,0:T(8,128)S(1)}) fusion(f32[32,256,128]{2,1,0:T(8,128)} %fusion.31, f32[32,256,128]{2,1,0:T(8,128)} %convolution_add_fusion.1, f32[32,256,128]{2,1,0:T(8,128)} %fusion.34, f32[32,256,128]{2,1,0:T(8,128)} %fusion.53, f32[128,32,256]{2,0,1:T(8,128)S(1)} %fusion.71, ...), kind=kOutput, calls=%fused_computation.44 | convolution fusion | flops 1622376448 | bytes 33816576 | tf_op jit(solution)/shard_map/jm,ckj->ckm/dot_general | solution.py:23
  727.4 4.9 convolution_add_fusion
  732.3 4.2 convolution_subtract_fusion
  740.7 5.7 multiply_bitcast_fusion
  749.5 35.4 %all_to_all.37 = f32[128,128,32]{1,2,0:T(8,128)} all-to-all(f32[128,128,32]{1,2,0:T(8,128)} %copy.185), channel_id=1, replica_groups=mesh['row'=16,'col'=8] {'row','col'}, dimensions={0} | all-to-all | bytes 4194304 | tf_op jit(solution)/shard_map/all_to_all | solution.py:124
  788.0 5.1 fusion.37
  (387 shorter events, 284.9 us)
Async XLA Ops:
  6.5 346.6 %all-gather.2.cloned.1.call-start = ((), (), s32[]{:S(2)}) async-start(), calls=%async_computation.3 | async-start | bytes 12681216 | tf_op jit(solution)/shard_map/all_gather | solution.py:31
  19.4 43.2 %all-to-all-start.1 = ((f32[128,128,32]{0,2,1:T(8,128)}), f32[128,128,32]{0,2,1:T(8,128)}, u32[]{:S(2)}, u32[]{:S(2)}) async-start(f32[128,128,32]{0,2,1:T(8,128)} %bitcast.366), calls=%async_computation.1 | async-start | bytes 4194304 | tf_op jit(solution)/shard_map/all_to_all | solution.py:121
  32.1 321.0 %copy-start.50 = (s32[128]{0:T(128)S(1)}, s32[128]{0:T(128)}, u32[]{:S(2)}) copy-start(s32[128]{0:T(128)} %param.7) | copy-start | bytes 1540
  361.9 13.4 %collective-permute-start = (bf16[6,12288]{1,0:T(8,128)(2,1)S(1)}, bf16[6,12288]{1,0:T(8,128)(2,1)S(1)}, u32[]{:S(2)}, u32[]{:S(2)}) collective-permute-start(bf16[6,12288]{1,0:T(8,128)(2,1)S(1)} %slice.72), channel_id=1, source_target_pairs={{0,1},{1,2},{2,3},{3,4},{4,5},{5,6},{6,7},{7,8},{8,9},{9,10},{10,1... | collective-permute-start | bytes 442376 | tf_op jit(solution)/shard_map/ppermute | solution.py:14
  518.3 85.5 %copy-start.11 = (f32[1,128,32]{1,2,0:T(8,128)S(1)}, f32[1,128,32]{1,2,0:T(8,128)}, u32[]{:S(2)}) copy-start(f32[1,128,32]{1,2,0:T(8,128)} %copy.130) | copy-start | bytes 49156
  518.3 86.1 %copy-start.40 = (f32[1,128,32]{1,2,0:T(8,128)S(1)}, f32[1,128,32]{1,2,0:T(8,128)}, u32[]{:S(2)}) copy-start(f32[1,128,32]{1,2,0:T(8,128)} %copy.131) | copy-start | bytes 49156
  518.3 86.6 %copy-start.38 = (f32[1,128,32]{1,2,0:T(8,128)S(1)}, f32[1,128,32]{1,2,0:T(8,128)}, u32[]{:S(2)}) copy-start(f32[1,128,32]{1,2,0:T(8,128)} %copy.132) | copy-start | bytes 49156
  518.3 87.3 %copy-start.36 = (f32[1,128,32]{1,2,0:T(8,128)S(1)}, f32[1,128,32]{1,2,0:T(8,128)}, u32[]{:S(2)}) copy-start(f32[1,128,32]{1,2,0:T(8,128)} %copy.133) | copy-start | bytes 49156
  518.3 87.9 %copy-start.34 = (f32[1,128,32]{1,2,0:T(8,128)S(1)}, f32[1,128,32]{1,2,0:T(8,128)}, u32[]{:S(2)}) copy-start(f32[1,128,32]{1,2,0:T(8,128)} %copy.134) | copy-start | bytes 49156
  518.4 88.4 %copy-start.32 = (f32[1,128,32]{1,2,0:T(8,128)S(1)}, f32[1,128,32]{1,2,0:T(8,128)}, u32[]{:S(2)}) copy-start(f32[1,128,32]{1,2,0:T(8,128)} %copy.135) | copy-start | bytes 49156
  518.4 89.0 %copy-start.30 = (f32[1,128,32]{1,2,0:T(8,128)S(1)}, f32[1,128,32]{1,2,0:T(8,128)}, u32[]{:S(2)}) copy-start(f32[1,128,32]{1,2,0:T(8,128)} %copy.136) | copy-start | bytes 49156
  518.4 89.6 %copy-start.28 = (f32[1,128,32]{1,2,0:T(8,128)S(1)}, f32[1,128,32]{1,2,0:T(8,128)}, u32[]{:S(2)}) copy-start(f32[1,128,32]{1,2,0:T(8,128)} %copy.137) | copy-start | bytes 49156
  518.5 90.1 %copy-start.26 = (f32[1,128,32]{1,2,0:T(8,128)S(1)}, f32[1,128,32]{1,2,0:T(8,128)}, u32[]{:S(2)}) copy-start(f32[1,128,32]{1,2,0:T(8,128)} %copy.138) | copy-start | bytes 49156
  518.5 90.7 %copy-start.24 = (f32[1,128,32]{1,2,0:T(8,128)S(1)}, f32[1,128,32]{1,2,0:T(8,128)}, u32[]{:S(2)}) copy-start(f32[1,128,32]{1,2,0:T(8,128)} %copy.139) | copy-start | bytes 49156
  518.6 91.2 %copy-start.22 = (f32[1,128,32]{1,2,0:T(8,128)S(1)}, f32[1,128,32]{1,2,0:T(8,128)}, u32[]{:S(2)}) copy-start(f32[1,128,32]{1,2,0:T(8,128)} %copy.140) | copy-start | bytes 49156
  518.6 91.8 %copy-start.20 = (f32[1,128,32]{1,2,0:T(8,128)S(1)}, f32[1,128,32]{1,2,0:T(8,128)}, u32[]{:S(2)}) copy-start(f32[1,128,32]{1,2,0:T(8,128)} %copy.141) | copy-start | bytes 49156
  518.6 92.4 %copy-start.18 = (f32[1,128,32]{1,2,0:T(8,128)S(1)}, f32[1,128,32]{1,2,0:T(8,128)}, u32[]{:S(2)}) copy-start(f32[1,128,32]{1,2,0:T(8,128)} %copy.142) | copy-start | bytes 49156
  518.7 93.0 %copy-start.16 = (f32[1,128,32]{1,2,0:T(8,128)S(1)}, f32[1,128,32]{1,2,0:T(8,128)}, u32[]{:S(2)}) copy-start(f32[1,128,32]{1,2,0:T(8,128)} %copy.143) | copy-start | bytes 49156
  518.7 93.6 %copy-start.14 = (f32[1,128,32]{1,2,0:T(8,128)S(1)}, f32[1,128,32]{1,2,0:T(8,128)}, u32[]{:S(2)}) copy-start(f32[1,128,32]{1,2,0:T(8,128)} %copy.144) | copy-start | bytes 49156
  518.7 94.1 %copy-start.12 = (f32[1,128,32]{1,2,0:T(8,128)S(1)}, f32[1,128,32]{1,2,0:T(8,128)}, u32[]{:S(2)}) copy-start(f32[1,128,32]{1,2,0:T(8,128)} %copy.145) | copy-start | bytes 49156
  518.7 94.7 %copy-start.10 = (f32[1,128,32]{1,2,0:T(8,128)S(1)}, f32[1,128,32]{1,2,0:T(8,128)}, u32[]{:S(2)}) copy-start(f32[1,128,32]{1,2,0:T(8,128)} %copy.146) | copy-start | bytes 49156
  518.7 95.3 %copy-start.9 = (f32[1,128,32]{1,2,0:T(8,128)S(1)}, f32[1,128,32]{1,2,0:T(8,128)}, u32[]{:S(2)}) copy-start(f32[1,128,32]{1,2,0:T(8,128)} %copy.147) | copy-start | bytes 49156
  518.8 95.8 %copy-start.8 = (f32[1,128,32]{1,2,0:T(8,128)S(1)}, f32[1,128,32]{1,2,0:T(8,128)}, u32[]{:S(2)}) copy-start(f32[1,128,32]{1,2,0:T(8,128)} %copy.148) | copy-start | bytes 49156
  627.3 40.9 %all-to-all-start = ((f32[128,128,32]{1,2,0:T(8,128)}), f32[128,128,32]{1,2,0:T(8,128)}, u32[]{:S(2)}, u32[]{:S(2)}) async-start(f32[128,128,32]{1,2,0:T(8,128)} %constant_dynamic-update-slice_fusion), calls=%async_computation | async-start | bytes 4194304 | tf_op jit(solution)/shard_map/all_to_all | solution.py:113
  (31 other events, 1650.4 us)
Sparse Core Ops, SparseCore 0:
  16.6 336.4 all-gather.1
